TPU v7x, 128 devices: a whole 4x4x4 slice. The times are simulated.
128 devices in a mesh: blk: 32 (over y_lo, x, z), cent: 4 (over y_hi, core).
Axes of the slice: x: 4, y: 4 (y_hi: 2, y_lo: 2; y = y_hi * 2 + y_lo), z: 4, core: 2. Of those that a mesh axis runs over, the one named last changes fastest.
Arguments:
- descriptors: bfloat16 [24576, 1024], P('blk'), may hold values from -6 to 6
- landmarks: bfloat16 [4096, 1024], P('blk'), may hold values from -6 to 6
- whitening: bfloat16 [4096, 4096], P('blk', 'cent'), may hold values from -0.09375 to 0.09375
- centroids: bfloat16 [4096, 4096], P('cent'), may hold values from -8 to 8, as said below
Outputs:
- assign: bfloat16 [24576, 4096], P('blk', 'cent')
- new_centroids: float32 [4096, 4096], P('blk', 'cent')
Inputs may be any that keep to these rules, and one draw needn't show every extreme that they name: `centroids`: centroid coordinates.
All inputs are finite; a program needn't handle non-finite values.
Results may differ from a plain program's by a relative error of at most 0.03.
Values may be sent and summed in bfloat16 or wider, within the bound.
A program may use at most 128 MiB of HBM per device.

v0:
```python
import math

import jax
import jax.numpy as jnp
from jax import lax
from jax.sharding import PartitionSpec as P


def unit_rows(values):
    wide = values.astype(jnp.float32)
    sum_sq = jnp.sum(wide * wide, axis=1, keepdims=True)
    scale = lax.rsqrt(sum_sq + 1e-06)
    return (wide * scale).astype(jnp.bfloat16)


def per_device(descriptors, landmarks, whitening, centroids):
    unit_desc = unit_rows(descriptors)
    unit_land = unit_rows(landmarks)
    sharpness = math.sqrt(descriptors.shape[1])
    cosine = lax.dot_general(
        unit_desc,
        lax.all_gather(unit_land, "blk", axis=0, tiled=True),
        (((1,), (1,)), ((), ())),
        preferred_element_type=jnp.float32,
    )
    kernel = jnp.exp(sharpness * cosine).astype(jnp.bfloat16)
    feature_cols = jnp.dot(
        kernel,
        lax.all_gather(whitening, "blk", axis=0, tiled=True),
        preferred_element_type=jnp.float32,
    )
    features = lax.all_gather(feature_cols.astype(jnp.bfloat16), "cent", axis=1, tiled=True)
    logits = lax.dot_general(
        features, centroids, (((1,), (1,)), ((), ())), preferred_element_type=jnp.float32
    )
    local_top = jnp.max(logits, axis=1)
    row_top = lax.pmax(local_top, "cent")
    weights = jnp.exp(logits - row_top[:, None])
    row_total = lax.psum(jnp.sum(weights, axis=1), "cent")
    assign = (weights / row_total[:, None]).astype(jnp.bfloat16)
    counts = lax.psum(jnp.sum(assign.astype(jnp.float32), axis=0), "blk")
    sums = lax.psum_scatter(
        lax.dot_general(
            features, assign, (((0,), (0,)), ((), ())), preferred_element_type=jnp.float32
        ).astype(jnp.bfloat16),
        "blk",
        scatter_dimension=0,
        tiled=True,
    ).astype(jnp.float32)
    return (assign, sums / jnp.maximum(counts, 1.0)[None, :])


def solution(mesh):
    in_specs = (P("blk", None), P("blk", None), P("blk", "cent"), P("cent", None))
    out_specs = (P("blk", "cent"), P("blk", "cent"))
    return jax.shard_map(
        per_device, mesh=mesh, in_specs=in_specs, out_specs=out_specs, check_vma=False
    )
```

profile of v0, /device:TPU:0, one launch (start us, length us, event | category | flops | bytes accessed | tf_op | source)
XLA Modules:
  0.0 652.7 jit_solution(8045331968475100106)
XLA Ops:
  7.2 0.0 all-gather.6.cloned.1.call-start
  7.2 0.7 all-gather.6.cloned.1.call-update
  7.9 0.0 all-gather.4.cloned.1.call-start
  7.9 1.1 fusion.8
  9.0 1.8 fusion.9
  10.8 0.0 all-gather.4.cloned.1.call-update
  10.8 0.0 all-gather.8.cloned.1.call-start
  10.9 1.8 fusion
  12.7 166.6 %all-gather.6.cloned.1.call-done = bf16[4096,1024]{1,0:T(8,128)(2,1)} async-done(((bf16[128,1024]{1,0:T(8,128)(2,1)}), bf16[4096,1024]{1,0:T(8,128)(2,1)}) %all-gather.6.cloned.1.call-update) | async-done | bytes 8388624 | tf_op jit(solution)/shard_map/all_gather | solution.py:29
  179.2 170.5 %all-gather.4.cloned.1.call-done = bf16[4096,1024]{1,0:T(8,128)(2,1)} async-done(((bf16[128,1024]{1,0:T(8,128)(2,1)}), bf16[4096,1024]{1,0:T(8,128)(2,1)}) %all-gather.4.cloned.1.call-update) | async-done | bytes 8388624 | tf_op jit(solution)/shard_map/all_gather | solution.py:22
  349.7 20.6 %convolution_convert_fusion.1 = bf16[768,1024]{1,0:T(8,128)(2,1)} fusion(bf16[4096,1024]{1,0:T(8,128)(2,1)} %all-gather.6.cloned.1.call-done, bf16[4096,1024]{1,0:T(8,128)(2,1)} %all-gather.4.cloned.1.call-done, bf16[768,1024]{1,0:T(8,128)(2,1)} %param.4, f32[768]{0:T(1024)S(1)} %add_rsqrt_fusion), kind=kOutput, calls=%fused_computation.10 | convolution fusion | flops 12894339072 | bytes 19926016 | tf_op jit(solution)/shard_map/dot_general | solution.py:27
  370.3 0.0 all-gather.8.cloned.1.call-update
  370.3 0.2 reduce-scatter.2.cloned.1.call-start
  370.6 51.5 %all-gather.8.cloned.1.call-done = bf16[768,4096]{1,0:T(8,128)(2,1)} async-done(((bf16[768,1024]{1,0:T(8,128)(2,1)}), bf16[768,4096]{1,0:T(8,128)(2,1)}) %all-gather.8.cloned.1.call-update) | async-done | bytes 6291472 | tf_op jit(solution)/shard_map/all_gather | solution.py:32
  422.0 11.1 %fusion.11 = (f32[768]{0:T(1024)S(1)}, f32[768,1024]{1,0:T(8,128)S(1)}) fusion(bf16[768,4096]{1,0:T(8,128)(2,1)} %all-gather.8.cloned.1.call-done, bf16[1024,4096]{1,0:T(8,128)(2,1)} %param.7), kind=kOutput, calls=%fused_computation.21 | convolution fusion | flops 6443236352 | bytes 17828864 | tf_op jit(solution)/shard_map/dot_general | solution.py:33
  433.1 7.4 %pmax.7 = f32[768]{0:T(1024)S(1)} all-reduce(f32[768]{0:T(1024)S(1)} %get-tuple-element.4), channel_id=1, replica_groups=mesh['blk'=32,'cent'=4] {'cent'}, use_global_device_ids=true, to_apply=%region_3.0 | all-reduce | flops 768 | bytes 6144 | tf_op jit(solution)/shard_map/pmax | solution.py:37
  440.6 0.9 fusion.2
  441.5 7.2 %psum.14 = f32[768]{0:T(1024)S(1)} all-reduce(f32[768]{0:T(1024)S(1)} %fusion.2), channel_id=1, replica_groups=mesh['blk'=32,'cent'=4] {'cent'}, use_global_device_ids=true, to_apply=%region_5.0 | all-reduce | flops 768 | bytes 6144 | tf_op jit(solution)/shard_map/psum | solution.py:39
  448.7 1.0 convert_reduce_fusion
  449.6 0.0 copy-start
  449.7 1.1 copy-done
  450.8 11.9 %convolution_convert_fusion = bf16[4096,1024]{1,0:T(8,128)(2,1)} fusion(bf16[768,4096]{1,0:T(8,128)(2,1)} %all-gather.8.cloned.1.call-done, bf16[768,1024]{1,0:T(8,128)(2,1)S(1)} %get-tuple-element.3), kind=kOutput, calls=%fused_computation.1 | convolution fusion | flops 6446645248 | bytes 16252928 | tf_op jit(solution)/shard_map/dot_general | solution.py:43
  462.6 0.0 reduce-scatter.2.cloned.1.call-update
  462.7 83.1 %psum.15 = f32[1024]{0:T(1024)S(1)} all-reduce(f32[1024]{0:T(1024)S(1)} %get-tuple-element.2), channel_id=1, replica_groups=mesh['blk'=32,'cent'=4] {'blk'}, use_global_device_ids=true, to_apply=%region_8.0 | all-reduce | flops 1024 | bytes 8192 | tf_op jit(solution)/shard_map/psum | solution.py:41
  545.7 98.6 %reduce-scatter.2.cloned.1.call-done = bf16[128,1024]{1,0:T(8,128)(2,1)} async-done(((bf16[4096,1024]{1,0:T(8,128)(2,1)}), bf16[128,1024]{1,0:T(8,128)(2,1)}) %reduce-scatter.2.cloned.1.call-update) | async-done | bytes 262160 | tf_op jit(solution)/shard_map/reduce_scatter | solution.py:42
  644.3 1.8 convert_divide_fusion
  (3 shorter events, 0.0 us)
Async XLA Ops:
  7.2 172.1 %all-gather.6.cloned.1.call-start = ((), (), s32[]{:S(2)}) async-start(), calls=%async_computation.2 | async-start | bytes 8650752 | tf_op jit(solution)/shard_map/all_gather | solution.py:29
  7.9 341.8 %all-gather.4.cloned.1.call-start = ((), (), s32[]{:S(2)}) async-start(), calls=%async_computation.1 | async-start | bytes 8650752 | tf_op jit(solution)/shard_map/all_gather | solution.py:22
  10.8 411.2 %all-gather.8.cloned.1.call-start = ((), (), s32[]{:S(2)}) async-start(), calls=%async_computation.3 | async-start | bytes 7864320 | tf_op jit(solution)/shard_map/all_gather | solution.py:32
  370.3 274.0 %reduce-scatter.2.cloned.1.call-start = ((), (), s32[]{:S(2)}) async-start(), calls=%async_computation.4 | async-start | bytes 8650752 | tf_op jit(solution)/shard_map/reduce_scatter | solution.py:42
  449.6 1.1 copy-start
Sparse Core Ops, SparseCore 0:
  9.6 169.5 all-gather.5
  181.5 168.1 all-gather.3
  370.4 51.5 all-gather.7
  462.8 181.4 reduce-scatter.1
where the time goes:
time: 653 us
  waiting for transfers between devices  488 us (75%)
  blocking collectives  97.7 us (15%)
  matrix products  43.6 us (7%)
  between operations  13.8 us (2%)
  other arithmetic  8.36 us (1%)
    all_gather x1, waiting for transfers between devices, per_device(): lax.all_gather(unit_land, 'blk', axis=0, tiled=True)  170 us
    all_gather x1, waiting for transfers between devices, per_device(): lax.all_gather(whitening, 'blk', axis=0, tiled=True)  167 us
    reduce_scatter x1, waiting for transfers between devices, per_device(): lax.psum_scatter(lax.dot_general(features, assign, (((0,), (0,)), ((), ()...  98.6 us
    psum x1, blocking collectives, per_device(): counts = lax.psum(jnp.sum(assign.astype(jnp.float32), axis=0), 'blk')  83.1 us
    all_gather x1, waiting for transfers between devices, per_device(): lax.all_gather(feature_cols.astype(jnp.bfloat16), 'cent', axis=1, tiled=T...  51.5 us
    dot_general x1, matrix products, per_device(): jnp.dot(kernel, lax.all_gather(whitening, 'blk', axis=0, tiled=True), pre...  20.6 us
  transfers between devices with their start and end apart: 4, of which 4 were waited for; matrix products, arithmetic and copies ran while one was open for 1% of the time, Pallas kernels for 0%

commit v1 on v0

v1 whole, which is shorter than its diff:
```python
import math

import jax
import jax.numpy as jnp
from jax import lax
from jax.experimental import pallas as pl
from jax.experimental.pallas import tpu as pltpu
from jax.sharding import PartitionSpec as P

MESH = pl.DeviceIdType.MESH
F32 = jnp.float32
BF16 = jnp.bfloat16

ROWS = 768
DEPTH = 1024
BLOCK = 128
GROUP = 4 * BLOCK
LAND = 8 * GROUP
HALF = 512
COLS = 1024
NSEM = 96


def dot(a, b, ca, cb):
    return lax.dot_general(a, b, (((ca,), (cb,)), ((), ())), preferred_element_type=F32)


def normalized(values):
    wide = values.astype(F32)
    sum_sq = jnp.sum(wide * wide, axis=1, keepdims=True)
    return (wide * lax.rsqrt(sum_sq + 1e-06)).astype(BF16)


def body(
    desc_hbm, land_hbm, white_hbm, cent_hbm, assign_hbm, out_hbm,
    desc, seed, land, white, kern, feat, cent, logit, assign_t,
    recv1, part1, recv2, part2, recv3, stat, count, out_v,
    send_sem, recv_sem, local_sem,
):
    blk, col = lax.axis_index("blk"), lax.axis_index("cent")
    y_lo, x, z = blk // 16, (blk // 4) % 4, blk % 4
    y_hi, core = col // 2, col % 2
    y = y_hi * 2 + y_lo
    away = (y_lo + core) % 2
    is_away, is_home = away == 1, away == 0

    def device(xx, yy, zz, cc):
        xx, yy, zz, cc = xx % 4, yy % 4, zz % 4, cc % 2
        return {"blk": (yy % 2) * 16 + xx * 4 + zz, "cent": (yy // 2) * 2 + cc}

    def on_a(d):
        return device(x + (1 - core) * (d + 4), y, z + core * (d + 4), core)

    def on_b(d):
        return device(x + core * (d + 4), y, z + (1 - core) * (d + 4), core)

    pa = x * (1 - core) + z * core
    pb = z * (1 - core) + x * core
    sibling = device(x, y, z, core + 1)
    swap_y = y + 1 - 2 * y_lo
    swap = device(x, swap_y, z, core + 1)
    other = device(x, 7 - y, z, core + 1)
    y_up, y_down = device(x, y + 1, z, core), device(x, y + 3, z, core)
    y_far, y_far_sib = device(x, y + 2, z, core), device(x, y + 2, z, core + 1)
    y_pair = device(x, swap_y, z, core)

    started = []
    counter = [0]

    def copy(src, dst, target, cond=None):
        k = counter[0]
        counter[0] += 1
        c = pltpu.make_async_remote_copy(
            src_ref=src, dst_ref=dst, send_sem=send_sem.at[k], recv_sem=recv_sem.at[k],
            device_id=target, device_id_type=MESH,
        )
        started.append((c, cond))
        return c

    def when(cond, f):
        pl.when(cond)(f)

    load_seed = pltpu.make_async_copy(land_hbm, seed, local_sem.at[0])
    load_desc = pltpu.make_async_copy(desc_hbm, desc.at[0], local_sem.at[1])
    load_seed.start()
    load_desc.start()
    load_cent = [
        pltpu.make_async_copy(cent_hbm.at[:, pl.ds(p * HALF, HALF)], cent.at[p], local_sem.at[2 + p])
        for p in range(8)
    ]
    load_white = [
        pltpu.make_async_copy(
            white_hbm.at[:, pl.ds(h * HALF, HALF)], white.at[h, pl.ds(0, BLOCK)], local_sem.at[10 + h]
        )
        for h in range(2)
    ]

    barrier = pltpu.get_barrier_semaphore()
    partners = [
        sibling, on_a(1), on_a(-1), on_a(2), on_b(1), on_b(-1), on_b(2),
        y_up, y_down, y_far, y_far_sib, swap, other,
    ]
    for target in partners:
        pl.semaphore_signal(barrier, inc=1, device_id=target, device_id_type=MESH)

    when(is_home, lambda: [c.start() for c in load_white] and None)
    load_seed.wait()
    seed[...] = normalized(seed[...])

    @pl.when(is_home)
    def _():
        land[pl.ds(0, BLOCK), :] = seed[...]

    pl.semaphore_wait(barrier, len(partners))

    swap_land = copy(seed, land.at[pl.ds(0, BLOCK)], swap, is_away)
    swap_white = [
        copy(white_hbm.at[:, pl.ds(h * HALF, HALF)], white.at[h, pl.ds(0, BLOCK)], swap, is_away)
        for h in range(2)
    ]
    CUT = 256
    swap_desc = [
        copy(desc.at[0, pl.ds(0, CUT)], desc.at[1, pl.ds(0, CUT)], swap, is_away),
        copy(desc.at[0, pl.ds(CUT, ROWS - CUT)], desc.at[1, pl.ds(CUT, ROWS - CUT)], other, is_away),
    ]

    class Ring:
        def __init__(self, at, size, to):
            def go(src, dst, rows, half, d):
                lo = half * (rows // 2)
                n = rows if half == 0 and dst != 2 else rows // 2
                return copy(at(src, lo, n), at(dst, lo, n), to(d))

            self.up = go(0, 3, size, 0, 1)
            self.down = go(0, 1, size, 0, -1)
            self.fwd_up = go(3, 2, size, 0, 1)
            self.fwd_down = go(1, 2, size, 1, -1)

    def land_a(slot, lo, n):
        return land.at[pl.ds(slot * BLOCK + lo, n)]

    def land_b(slot, lo, n):
        return land.at[pl.ds(slot * GROUP + lo, n)]

    def white_a(h):
        return lambda slot, lo, n: white.at[h, pl.ds(slot * BLOCK + lo, n)]

    def white_b(h):
        return lambda slot, lo, n: white.at[h, pl.ds(slot * GROUP + lo, n)]

    la = Ring(land_a, BLOCK, on_a)
    wa = [Ring(white_a(h), BLOCK, on_a) for h in range(2)]
    lb = Ring(land_b, GROUP, on_b)
    wb = [Ring(white_b(h), GROUP, on_b) for h in range(2)]

    def to_sibling(at, slot):
        return copy(at(slot, 0, GROUP), at(4 + slot, 0, GROUP), sibling)

    ls = [to_sibling(land_b, s) for s in range(4)]
    ws = [[to_sibling(white_b(h), s) for s in range(4)] for h in range(2)]

    @pl.when(is_home)
    def _():
        la.up.start()
        la.down.start()
        for h in range(2):
            load_white[h].wait()
            wa[h].up.start()
            wa[h].down.start()

    @pl.when(is_away)
    def _():
        swap_land.start()
        for h in range(2):
            swap_white[h].start()

    load_desc.wait()

    @pl.loop(0, 3)
    def _(i):
        s = pl.ds(pl.multiple_of(i * 256, 256), 256)
        desc[0, s, :] = normalized(desc[0, s, :])

    @pl.when(is_away)
    def _():
        swap_desc[0].start()
        swap_desc[1].start()
        swap_land.wait_recv()
        la.up.start()
        la.down.start()
        for h in range(2):
            swap_white[h].wait_recv()
            wa[h].up.start()
            wa[h].down.start()

    def forward(ring):
        ring.up.wait_recv()
        ring.fwd_up.start()
        ring.down.wait_recv()
        ring.fwd_down.start()

    def finish(ring):
        ring.fwd_up.wait_recv()
        ring.fwd_down.wait_recv()

    def stage2(ring, sib):
        ring.up.start()
        ring.down.start()
        sib[0].start()

    def stage2_forward(ring, sib):
        forward(ring)
        sib[3].start()
        sib[1].start()

    for c in load_cent:
        c.start()

    sharpness = math.sqrt(DEPTH)

    def kernel_group(g):
        cols = pl.ds(g * GROUP, GROUP)
        cosine = dot(desc[away], land[cols, :], 1, 1)
        kern[:, cols] = jnp.exp(sharpness * cosine).astype(BF16)

    forward(la)
    finish(la)
    stage2(lb, ls)
    forward(wa[0])
    forward(wa[1])

    @pl.when(is_away)
    def _():
        swap_desc[0].wait_recv()
        swap_desc[1].wait_recv()

    kernel_group(0)
    ls[0].wait_recv()
    kernel_group(4)
    finish(wa[0])
    finish(wa[1])
    stage2_forward(lb, ls)
    stage2(wb[0], ws[0])
    kernel_group(3)
    kernel_group(1)
    ls[3].wait_recv()
    kernel_group(7)
    ls[1].wait_recv()
    kernel_group(5)
    finish(lb)
    ls[2].start()
    kernel_group(2)
    stage2_forward(wb[0], ws[0])
    stage2(wb[1], ws[1])
    ls[2].wait_recv()
    kernel_group(6)
    finish(wb[0])
    ws[0][2].start()

    def features(h):
        for s in range(4):
            ws[h][s].wait_recv()
        slot = (1 - away) * (y * 2 + h) + away * (8 + h)

        @pl.loop(0, 3)
        def _(i):
            s = pl.ds(pl.multiple_of(i * 256, 256), 256)
            feat[slot, s, :] = dot(kern[s, :], white[h], 1, 0).astype(BF16)

    own = [y * 2 + h for h in range(2)]
    f_far = [copy(feat.at[own[h]], feat.at[own[h]], y_far, is_home) for h in range(2)]
    f_up = [copy(feat.at[8 + h], feat.at[own[h]], y_up, is_away) for h in range(2)]
    f_down = [copy(feat.at[8 + h], feat.at[own[h]], y_down, is_away) for h in range(2)]

    def slot_of(r, h):
        return ((y + r) % 4) * 2 + h

    f_sib = [
        [copy(feat.at[slot_of(r, h)], feat.at[slot_of(r, h)], sibling, is_home) for r in range(4)]
        for h in range(2)
    ]

    def send_features(h):
        @pl.when(is_home)
        def _():
            f_far[h].start()
            f_sib[h][0].start()

        @pl.when(is_away)
        def _():
            f_up[h].start()
            f_down[h].start()

    features(0)
    send_features(0)
    stage2_forward(wb[1], ws[1])
    finish(wb[1])
    ws[1][2].start()
    features(1)
    send_features(1)

    for c in load_cent:
        c.wait()
    arrived = {1: f_down, 3: f_up, 2: f_far}
    for h in range(2):
        for r in (0, 1, 3, 2):
            if r == 0:
                when(is_away, lambda h=h: f_sib[h][0].wait_recv())
            else:

                @pl.when(is_home)
                def _(h=h, r=r):
                    arrived[r][h].wait_recv()
                    f_sib[h][r].start()

                when(is_away, lambda h=h, r=r: f_sib[h][r].wait_recv())
            slot = slot_of(r, h)
            update = dot(cent[slot], feat[slot], 1, 1)
            if h == 0 and r == 0:
                logit[...] = update
            else:
                logit[...] += update

    top = jnp.max(logit[...], axis=0, keepdims=True)
    weights = jnp.exp(logit[...] - top)
    logit[...] = weights
    total = jnp.sum(weights, axis=0, keepdims=True)
    stat[0, 0:1, :] = top
    stat[0, 1:2, :] = total
    stat_copies = [
        copy(stat.at[0], stat.at[i + 1], target)
        for i, target in enumerate((sibling, y_far, y_far_sib))
    ]
    for c in stat_copies:
        c.start()
    for c in stat_copies:
        c.wait_recv()
    tops = [stat[i, 0:1, :] for i in range(4)]
    all_top = jnp.maximum(jnp.maximum(tops[0], tops[1]), jnp.maximum(tops[2], tops[3]))
    all_total = sum(stat[i, 1:2, :] * jnp.exp(tops[i] - all_top) for i in range(4))
    factor = jnp.exp(tops[0] - all_top) / all_total
    assign_t[...] = (logit[...] * factor).astype(BF16)

    def partial_sum(ta, yy):
        ta = ta % 4
        parts = []
        for b in range(4):
            xb = (1 - core) * ta + core * b
            zb = (1 - core) * b + core * ta
            lanes = pl.ds(pl.multiple_of(zb * 128, 128), 128)
            parts.append(feat[yy * 4 + xb, :, lanes])
        return dot(assign_t[...], jnp.concatenate(parts, axis=1), 1, 0)

    X0, X1, Y0, Y1, Z0, Z1 = range(6)
    rs1 = [
        copy(cent.at[0], recv1.at[X0], on_a(1)),
        copy(cent.at[1], recv1.at[X1], on_a(-1)),
        copy(cent.at[2], recv1.at[Y1], on_a(1)),
        copy(cent.at[3], recv1.at[Y0], on_a(-1)),
        copy(cent.at[4], recv1.at[Z0], on_a(1)),
        copy(cent.at[5], recv1.at[Z1], on_a(-1)),
    ]
    cent[0] = partial_sum(pa + 2, 0).astype(BF16)
    rs1[0].start()
    cent[1] = partial_sum(pa + 2, 1).astype(BF16)
    rs1[1].start()
    cent[2] = partial_sum(pa + 1, 1).astype(BF16)
    rs1[2].start()
    cent[3] = partial_sum(pa + 3, 0).astype(BF16)
    rs1[3].start()

    ones = jnp.ones((8, ROWS), BF16)
    count[0] = dot(ones, assign_t[...], 1, 1)
    count_a = [copy(count.at[0], count.at[1 + i], on_a(d)) for i, d in enumerate((1, -1, 2))]
    count_b = [copy(count.at[4], count.at[5 + i], on_b(d)) for i, d in enumerate((1, -1, 2))]
    count_y = copy(count.at[8], count.at[9], y_pair)
    for c in count_a:
        c.start()

    cent[4] = partial_sum(pa + 1, 0).astype(BF16)
    cent[5] = partial_sum(pa + 3, 1).astype(BF16)
    cent[6] = partial_sum(pa, 0).astype(BF16)
    cent[7] = partial_sum(pa, 1).astype(BF16)

    @pl.when(is_away)
    def _():
        swap_desc[0].wait_send()
        swap_desc[1].wait_send()

    @pl.loop(0, 6)
    def _(i):
        s = pl.ds(pl.multiple_of(i * 128, 128), 128)
        desc[0, s, :] = assign_t[:, s].T

    store_assign = pltpu.make_async_copy(desc.at[0], assign_hbm, local_sem.at[12])
    store_assign.start()

    for c in count_a:
        c.wait_recv()
    count[4] = count[0] + count[1] + count[2] + count[3]
    for c in count_b:
        c.start()

    rs1[0].wait_recv()
    cent[4] = (cent[4].astype(F32) + recv1[X0].astype(F32)).astype(BF16)
    rs1[4].start()
    rs1[1].wait_recv()
    cent[5] = (cent[5].astype(F32) + recv1[X1].astype(F32)).astype(BF16)
    rs1[5].start()

    for c in count_b:
        c.wait_recv()
    count[8] = count[4] + count[5] + count[6] + count[7]
    count_y.start()

    rs1[2].wait_recv()
    rs1[3].wait_recv()
    up, down, far = (pb + 1) % 4, (pb + 3) % 4, (pb + 2) % 4
    rs1[4].wait_recv()
    for b in range(4):
        s = pl.ds(b * 128, 128)
        total = cent[6, :, s].astype(F32) + recv1[Y0, :, s].astype(F32) + recv1[Z0, :, s].astype(F32)
        part1[b] = total.astype(BF16)
    rs1[5].wait_recv()
    for b in range(4):
        s = pl.ds(b * 128, 128)
        total = cent[7, :, s].astype(F32) + recv1[Y1, :, s].astype(F32) + recv1[Z1, :, s].astype(F32)
        part1[4 + b] = total.astype(BF16)

    rs2 = [
        copy(part1.at[far], recv2.at[X0], on_b(1)),
        copy(part1.at[4 + far], recv2.at[X1], on_b(-1)),
        copy(part1.at[4 + up], recv2.at[Y1], on_b(1)),
        copy(part1.at[down], recv2.at[Y0], on_b(-1)),
        copy(part2.at[0], recv2.at[Z0], on_b(1)),
        copy(part2.at[1], recv2.at[Z1], on_b(-1)),
    ]
    for c in rs2[:4]:
        c.start()
    rs2[0].wait_recv()
    part2[0] = (part1[up].astype(F32) + recv2[X0].astype(F32)).astype(BF16)
    rs2[4].start()
    rs2[1].wait_recv()
    part2[1] = (part1[4 + down].astype(F32) + recv2[X1].astype(F32)).astype(BF16)
    rs2[5].start()
    for c in rs2[2:]:
        c.wait_recv()

    part2[2] = (part1[pb].astype(F32) + recv2[Y0].astype(F32) + recv2[Z0].astype(F32)).astype(BF16)
    part2[3] = (part1[4 + pb].astype(F32) + recv2[Y1].astype(F32) + recv2[Z1].astype(F32)).astype(BF16)
    rs3 = copy(part2.at[3 - y_lo], recv3, y_pair)
    rs3.start()
    count_y.wait_recv()
    counts = count[8, 0:1, :] + count[9, 0:1, :]
    rs3.wait_recv()
    sums = part2[2 + y_lo].astype(F32) + recv3[...].astype(F32)
    out_v[...] = sums.T / jnp.maximum(counts, 1.0)
    store_out = pltpu.make_async_copy(out_v, out_hbm, local_sem.at[13])
    store_out.start()

    for c, cond in started:
        if any(c is d for d in swap_desc):
            continue
        if cond is None:
            c.wait_send()
        else:
            when(cond, lambda c=c: c.wait_send())
    store_assign.wait()
    store_out.wait()


def per_device(descriptors, landmarks, whitening, centroids):
    vmem = pltpu.VMEM
    hbm = pl.BlockSpec(memory_space=pl.ANY)
    flops = 2 * ROWS * LAND * DEPTH * 4
    return pl.pallas_call(
        body,
        out_shape=(
            jax.ShapeDtypeStruct((ROWS, COLS), BF16),
            jax.ShapeDtypeStruct((BLOCK, COLS), F32),
        ),
        in_specs=[hbm] * 4,
        out_specs=(hbm, hbm),
        scratch_shapes=[
            vmem((2, ROWS, DEPTH), BF16),
            vmem((BLOCK, DEPTH), BF16),
            vmem((LAND, DEPTH), BF16),
            vmem((2, LAND, HALF), BF16),
            vmem((ROWS, LAND), BF16),
            vmem((10, ROWS, HALF), BF16),
            vmem((8, COLS, HALF), BF16),
            vmem((COLS, ROWS), F32),
            vmem((COLS, ROWS), BF16),
            vmem((6, COLS, HALF), BF16),
            vmem((8, COLS, 128), BF16),
            vmem((6, COLS, 128), BF16),
            vmem((4, COLS, 128), BF16),
            vmem((COLS, 128), BF16),
            vmem((4, 8, ROWS), F32),
            vmem((10, 8, COLS), F32),
            vmem((BLOCK, COLS), F32),
            pltpu.SemaphoreType.DMA((NSEM,)),
            pltpu.SemaphoreType.DMA((NSEM,)),
            pltpu.SemaphoreType.DMA((16,)),
        ],
        compiler_params=pltpu.CompilerParams(
            collective_id=0, has_side_effects=True, vmem_limit_bytes=62 << 20
        ),
        cost_estimate=pl.CostEstimate(flops=flops, bytes_accessed=16 << 20, transcendentals=0),
        name="kmeans_step",
    )(descriptors, landmarks, whitening, centroids)


def solution(mesh):
    in_specs = (P("blk", None), P("blk", None), P("blk", "cent"), P("cent", None))
    out_specs = (P("blk", "cent"), P("blk", "cent"))
    return jax.shard_map(
        per_device, mesh=mesh, in_specs=in_specs, out_specs=out_specs, check_vma=False
    )
```

time: 653 us -> 177 us (0.27)
  the two profiles are of different devices: /device:TPU:0 before, /device:TPU:1 now
where the time goes in v1:
time: 177 us; the launch traced here: 175 us
  Pallas kernels  171 us (97%)
  local copies, waits for them, and re-layouts  3.52 us (2%)
    pallas_call x1, Pallas kernels, per_device(): pl.pallas_call(body, out_shape=(jax.ShapeDtypeStruct((ROWS, COLS), BF16),...  171 us

profile of v1, /device:TPU:1, one launch (start us, length us, event | category | flops | bytes accessed | tf_op | source)
XLA Modules:
  0.0 174.8 jit_solution(8780069714172847511)
XLA Ops:
  0.6 170.6 %kmeans_step.1 = (bf16[768,1024]{1,0:T(8,128)(2,1)}, f32[128,1024]{1,0:T(8,128)}) custom-call(bf16[768,1024]{1,0:T(8,128)(2,1)} %desc_hbm.1, bf16[128,1024]{1,0:T(8,128)(2,1)} %land_hbm.1, bf16[128,1024]{1,0:T(8,128)(2,1)} %white_hbm.1, bf16[1024,4096]{1,0:T(8,128)(2,1)} %cent_hbm.1), custom_call_target="tpu_custom_call" | custom-call | flops 25769803776 | bytes 16777216 | tf_op jit(solution)/shard_map/kmeans_step/pallas_call | solution.py:476
  171.2 0.0 copy-start
  171.2 2.7 %copy.8 = bf16[768,1024]{1,0:T(8,128)(2,1)} copy(bf16[768,1024]{1,0:T(8,128)(2,1)} %get-tuple-element.4) | data formatting | bytes 3145728
  174.0 0.0 copy-done
  174.0 0.8 copy.9
Async XLA Ops:
  171.2 2.7 %copy-start = (f32[128,1024]{1,0:T(8,128)S(1)}, f32[128,1024]{1,0:T(8,128)}, u32[]{:S(2)}) copy-start(f32[128,1024]{1,0:T(8,128)} %get-tuple-element.5) | copy-start | bytes 1572868

commit v2 on v1

v2 whole, which is shorter than its diff:
```python
import math

import jax
import jax.numpy as jnp
from jax import lax
from jax.experimental import pallas as pl
from jax.experimental.pallas import tpu as pltpu
from jax.sharding import PartitionSpec as P

MESH = pl.DeviceIdType.MESH
F32 = jnp.float32
BF16 = jnp.bfloat16

ROWS = 768
DEPTH = 1024
BLOCK = 128
SUB = 64
HALF_B = 256
GROUP = 4 * BLOCK
LAND = 8 * GROUP
HALF = 512
PIECE = 256
CHUNKS = 4
WCHUNKS = 8
PART = 256
COLS = 1024
NSEM = 224


def dot(a, b, ca, cb):
    return lax.dot_general(a, b, (((ca,), (cb,)), ((), ())), preferred_element_type=F32)


def normalized(values):
    wide = values.astype(F32)
    sum_sq = jnp.sum(wide * wide, axis=1, keepdims=True)
    return (wide * lax.rsqrt(sum_sq + 1e-06)).astype(BF16)


def body(
    desc_hbm, land_hbm, white_hbm, cent_hbm, assign_hbm, out_hbm,
    desc, seed, wseed, land, white, kern, feat, cent, logit, assign_t,
    recv1, part1, recv2, stat, count, out_v,
    send_sem, recv_sem, local_sem, free_sem,
):
    blk, col = lax.axis_index("blk"), lax.axis_index("cent")
    y_lo, x, z = blk // 16, (blk // 4) % 4, blk % 4
    y_hi, core = col // 2, col % 2
    y = y_hi * 2 + y_lo
    away = (y_lo + core) % 2
    is_away, is_home = away == 1, away == 0

    def device(xx, yy, zz, cc):
        xx, yy, zz, cc = xx % 4, yy % 4, zz % 4, cc % 2
        return {"blk": (yy % 2) * 16 + xx * 4 + zz, "cent": (yy // 2) * 2 + cc}

    def on_a(d):
        return device(x + (1 - core) * (d + 4), y, z + core * (d + 4), core)

    def on_b(d):
        return device(x + core * (d + 4), y, z + (1 - core) * (d + 4), core)

    pa = x * (1 - core) + z * core
    pb = z * (1 - core) + x * core
    sibling = device(x, y, z, core + 1)
    swap_y = y + 1 - 2 * y_lo
    swap = device(x, swap_y, z, core + 1)
    other = device(x, 7 - y, z, core + 1)
    y_up, y_down = device(x, y + 1, z, core), device(x, y + 3, z, core)
    y_far, y_far_sib = device(x, y + 2, z, core), device(x, y + 2, z, core + 1)
    y_pair, other_same = device(x, swap_y, z, core), device(x, 7 - y, z, core)

    started = []
    counter = [0]

    def wait_send(c):
        for i, (other_copy, cond) in enumerate(started):
            if other_copy is c:
                del started[i]
                if cond is None:
                    c.wait_send()
                else:
                    pl.when(cond)(c.wait_send)
                return

    def copy(src, dst, target, cond=None):
        k = counter[0]
        counter[0] += 1
        c = pltpu.make_async_remote_copy(
            src_ref=src, dst_ref=dst, send_sem=send_sem.at[k], recv_sem=recv_sem.at[k],
            device_id=target, device_id_type=MESH,
        )
        started.append((c, cond))
        return c

    def when(cond, f):
        pl.when(cond)(f)

    load_seed = pltpu.make_async_copy(land_hbm, seed, local_sem.at[0])
    load_desc = pltpu.make_async_copy(desc_hbm, desc.at[0], local_sem.at[1])
    load_seed.start()
    load_desc.start()
    load_cent = [
        pltpu.make_async_copy(cent_hbm.at[:, pl.ds(p * HALF, HALF)], cent.at[p], local_sem.at[2 + p])
        for p in range(8)
    ]
    load_white = [
        pltpu.make_async_copy(white_hbm.at[:, pl.ds(k * PIECE, PIECE)], wseed.at[k], local_sem.at[10 + k])
        for k in range(CHUNKS)
    ]
    for c in load_white:
        c.start()

    barrier = pltpu.get_barrier_semaphore()
    partners = [
        sibling, on_a(1), on_a(-1), on_a(2), on_b(1), on_b(-1), on_b(2),
        y_up, y_down, y_far, y_far_sib, swap, other,
    ]
    for target in partners:
        pl.semaphore_signal(barrier, inc=1, device_id=target, device_id_type=MESH)

    load_seed.wait()
    seed[...] = normalized(seed[...])
    mine = pl.ds(pl.multiple_of(core * SUB, SUB), SUB)
    theirs = pl.ds(pl.multiple_of((1 - core) * SUB, SUB), SUB)
    land[pl.ds(0, SUB), :] = seed[mine, :]

    pl.semaphore_wait(barrier, len(partners))

    swap_land = copy(seed.at[mine], land.at[pl.ds(HALF_B, SUB)], y_pair)

    def white_seed(quarter, part, rows, target, cond):
        return copy(
            wseed.at[:, rows], white.at[pl.ds(quarter * CHUNKS, CHUNKS), pl.ds(part * HALF_B, SUB)], target, cond
        )

    seed_own = pltpu.make_async_copy(
        wseed.at[:, mine], white.at[pl.ds(0, CHUNKS), pl.ds(0, SUB)], local_sem.at[15]
    )
    seed_sib = white_seed(0, 0, theirs, sibling, is_home)
    seed_pair = white_seed(0, 1, mine, y_pair, is_away)
    seed_swap = white_seed(0, 1, theirs, swap, is_away)
    seed_far = white_seed(1, 0, mine, y_far, is_home)
    seed_far_sib = white_seed(1, 0, theirs, y_far_sib, is_home)
    seed_other = white_seed(1, 1, theirs, other, is_away)
    seed_other_same = white_seed(1, 1, mine, other_same, is_away)
    CUT = 256
    share_cent = [
        copy(cent_hbm.at[:, pl.ds(p * HALF, HALF)], cent.at[p], sibling, is_home) for p in range(8)
    ]
    swap_desc = [
        copy(desc.at[0, pl.ds(0, CUT)], desc.at[1, pl.ds(0, CUT)], swap, is_away),
        copy(desc.at[0, pl.ds(CUT, ROWS - CUT)], desc.at[1, pl.ds(CUT, ROWS - CUT)], other, is_away),
    ]

    class Ring:
        def __init__(self, at, size, to):
            def go(src, dst, rows, half, d):
                lo = half * (rows // 2)
                n = rows if half == 0 and dst != 2 else rows // 2
                return copy(at(src, lo, n), at(dst, lo, n), to(d))

            self.up = go(0, 3, size, 0, 1)
            self.down = go(0, 1, size, 0, -1)
            self.fwd_up = go(3, 2, size, 0, 1)
            self.fwd_down = go(1, 2, size, 1, -1)

        def start(self):
            self.up.start()
            self.down.start()

        def forward(self):
            self.up.wait_recv()
            self.fwd_up.start()
            self.down.wait_recv()
            self.fwd_down.start()

        def finish(self):
            self.fwd_up.wait_recv()
            self.fwd_down.wait_recv()

    def land_a(part):
        return lambda slot, lo, n: land.at[pl.ds(part * HALF_B + slot * SUB + lo, n)]

    def land_b(first):
        return lambda slot, lo, n: land.at[pl.ds(slot * GROUP + first + lo, n)]

    def white_a(quarter, part):
        return lambda slot, lo, n: white.at[
            pl.ds(quarter * CHUNKS, CHUNKS), pl.ds(part * HALF_B + slot * SUB + lo, n)
        ]

    def white_b(k):
        return lambda slot, lo, n: white.at[k, pl.ds(slot * GROUP + lo, n)]

    def to_sibling(at, slot):
        return copy(at(slot, 0, GROUP), at(4 + slot, 0, GROUP), sibling)

    la = [Ring(land_a(part), SUB, on_a) for part in range(2)]
    lb = [Ring(land_b(s * SUB), SUB, on_b) for s in range(4)]
    lb_rest = Ring(land_b(HALF_B), HALF_B, on_b)
    wa = [[Ring(white_a(q, part), SUB, on_a) for part in range(2)] for q in range(2)]
    wb = [Ring(white_b(k), GROUP, on_b) for k in range(WCHUNKS)]
    ls = [to_sibling(land_b(0), s) for s in range(4)]
    ws = [[to_sibling(white_b(k), s) for s in range(4)] for k in range(WCHUNKS)]

    swap_land.start()
    la[0].start()
    lb[0].start()
    for c in load_white:
        c.wait()

    @pl.when(is_home)
    def _():
        seed_own.start()
        seed_sib.start()

    @pl.when(is_away)
    def _():
        seed_pair.start()
        seed_swap.start()

    load_desc.wait()

    @pl.loop(0, 3)
    def _(i):
        s = pl.ds(pl.multiple_of(i * 256, 256), 256)
        desc[0, s, :] = normalized(desc[0, s, :])

    @pl.when(is_away)
    def _():
        swap_desc[0].start()
        swap_desc[1].start()
        seed_other.start()
        seed_other_same.start()

    @pl.when(is_home)
    def _():
        seed_far.start()
        seed_far_sib.start()
        for c in load_cent + share_cent:
            c.start()

    sharpness = math.sqrt(DEPTH)

    def kernel_group(g):
        cols = pl.ds(g * GROUP, GROUP)
        cosine = dot(desc[away], land[cols, :], 1, 1)
        kern[:, cols] = jnp.exp(sharpness * cosine).astype(BF16)

    la[0].up.wait_recv()
    la[0].fwd_up.start()
    lb[3].start()
    la[0].down.wait_recv()
    la[0].fwd_down.start()
    lb[1].start()
    swap_land.wait_recv()
    la[1].start()
    lb[0].forward()
    la[0].finish()
    lb[2].start()
    lb[3].forward()
    lb[1].forward()
    la[1].forward()

    @pl.when(is_home)
    def _():
        seed_own.wait()
        seed_pair.wait_recv()

    @pl.when(is_away)
    def _():
        seed_sib.wait_recv()
        seed_swap.wait_recv()

    for ring in wa[0]:
        ring.start()
    lb[2].forward()
    la[1].finish()
    lb_rest.start()
    ls[0].start()

    @pl.when(is_away)
    def _():
        swap_desc[0].wait_recv()
        swap_desc[1].wait_recv()

    kernel_group(0)
    for ring in wa[0]:
        ring.forward()
    for ring in lb:
        ring.finish()
    lb_rest.forward()
    ls[3].start()
    ls[1].start()
    for ring in wa[0]:
        ring.finish()

    def start_white(k):
        wb[k].start()
        ws[k][0].start()

    def forward_white(k):
        wb[k].forward()
        ws[k][3].start()
        ws[k][1].start()

    def finish_white(k):
        wb[k].finish()
        ws[k][2].start()

    start_white(0)
    start_white(1)
    kernel_group(3)
    kernel_group(1)
    lb_rest.finish()
    ls[2].start()

    @pl.when(is_home)
    def _():
        seed_far.wait_recv()
        seed_other_same.wait_recv()

    @pl.when(is_away)
    def _():
        seed_far_sib.wait_recv()
        seed_other.wait_recv()

    for ring in wa[1]:
        ring.start()
    ls[0].wait_recv()
    kernel_group(4)
    forward_white(0)
    start_white(2)
    ls[3].wait_recv()
    kernel_group(7)
    ls[1].wait_recv()
    kernel_group(5)
    kernel_group(2)
    finish_white(0)
    for ring in wa[1]:
        ring.forward()
    forward_white(1)
    start_white(3)
    ls[2].wait_recv()
    kernel_group(6)

    def slot_of(r, k):
        return ((y + r) % 4) * CHUNKS + k

    def features(k):
        for s in range(4):
            ws[k][s].wait_recv()
        slot = slot_of(0, k) if k < CHUNKS else slot_of(2, k - CHUNKS)

        @pl.loop(0, 3)
        def _(i):
            s = pl.ds(pl.multiple_of(i * 256, 256), 256)
            feat[slot, s, :] = dot(kern[s, :], white[k], 1, 0).astype(BF16)

    own = [feat.at[slot_of(0, k)] for k in range(CHUNKS)]
    f_up = [copy(own[k], own[k], y_up) for k in range(CHUNKS)]
    f_down = [copy(own[k], own[k], y_down) for k in range(CHUNKS)]

    def logits(r, k):
        if r == 1:
            f_down[k].wait_recv()
        if r == 3:
            f_up[k].wait_recv()
        lanes = pl.ds((k % 2) * PIECE, PIECE)
        slot, piece = ((y + r) % 4) * 2 + k // 2, slot_of(r, k)

        @pl.loop(0, 2)
        def _(i):
            s = pl.ds(pl.multiple_of(i * 512, 512), 512)
            update = dot(cent[slot, s, lanes], feat[piece], 1, 1)
            if k == 0 and r == 0:
                logit[s, :] = update
            else:
                logit[s, :] += update

    features(0)
    f_up[0].start()
    f_down[0].start()
    for k in range(1, CHUNKS):
        finish_white(k)
        if k == 1:
            for ring in wa[1]:
                ring.finish()
        forward_white(k + 1)
        start_white(k + 3)
        features(k)
        f_up[k].start()
        f_down[k].start()

    @pl.when(is_home)
    def _():
        for c in load_cent:
            c.wait()

    @pl.when(is_away)
    def _():
        for c in share_cent:
            c.wait_recv()

    todo = [
        [(0, 0), (0, 1)],
        [(0, 2), (0, 3), (2, 0)],
        [(1, 0), (3, 0), (2, 1)],
        [(1, 1), (3, 1), (2, 2), (1, 2), (3, 2), (2, 3), (1, 3), (3, 3)],
    ]
    for k in range(CHUNKS, WCHUNKS):
        finish_white(k)
        if k + 1 < WCHUNKS:
            forward_white(k + 1)
        if k + 3 < WCHUNKS:
            start_white(k + 3)
        features(k)
        for r, piece in todo[k - CHUNKS]:
            logits(r, piece)

    for ring in la + lb + [lb_rest]:
        for c in (ring.up, ring.down, ring.fwd_up, ring.fwd_down):
            wait_send(c)
    for c in ls:
        wait_send(c)
    pl.semaphore_signal(free_sem, inc=1, device_id=sibling, device_id_type=MESH)

    def quarter(i):
        return pl.ds(pl.multiple_of(i * 256, 256), 256)

    def highest(i, top):
        return jnp.maximum(top, jnp.max(logit[quarter(i), :], axis=0, keepdims=True))

    top = lax.fori_loop(0, 4, highest, jnp.full((1, ROWS), -jnp.inf, F32))

    def exponentials(i, total):
        weights = jnp.exp(logit[quarter(i), :] - top)
        logit[quarter(i), :] = weights
        return total + jnp.sum(weights, axis=0, keepdims=True)

    total = lax.fori_loop(0, 4, exponentials, jnp.zeros((1, ROWS), F32))
    stat[0, 0:1, :] = top
    stat[0, 1:2, :] = total
    stat_copies = [
        copy(stat.at[0], stat.at[i + 1], target)
        for i, target in enumerate((y_up, y_down, y_far))
    ]
    for c in stat_copies:
        c.start()
    for c in stat_copies:
        c.wait_recv()
    tops = [stat[i, 0:1, :] for i in range(4)]
    all_top = jnp.maximum(jnp.maximum(tops[0], tops[1]), jnp.maximum(tops[2], tops[3]))
    all_total = sum(stat[i, 1:2, :] * jnp.exp(tops[i] - all_top) for i in range(4))
    factor = jnp.exp(tops[0] - all_top) / all_total

    @pl.loop(0, 4)
    def _(i):
        assign_t[quarter(i), :] = (logit[quarter(i), :] * factor).astype(BF16)

    def partial_sum(slot, ta, owner, i):
        ta = ta % 4
        parts = []
        for b in range(4):
            xb = (1 - owner) * ta + owner * b
            zb = (1 - owner) * b + owner * ta
            lanes = pl.ds(pl.multiple_of((zb % 2) * 128, 128), 128)
            parts.append(feat[(owner * 4 + xb) * 2 + zb // 2, :, lanes])
        s = pl.ds(i * 512, 512)
        cent[slot, s, :] = dot(assign_t[s, :], jnp.concatenate(parts, axis=1), 1, 0).astype(BF16)

    def add(*values):
        total = values[0].astype(F32)
        for v in values[1:]:
            total = total + v.astype(F32)
        return total

    FAR, UP, DOWN, OWN = range(4)
    offsets = (2, 1, 3, 0)
    landing = [land.at[pl.ds(t * COLS, COLS), pl.ds(0, HALF)] for t in range(4)]
    halves = [
        [copy(cent.at[4 + t, rows], landing[t].at[rows], sibling) for rows in (pl.ds(0, 512), pl.ds(512, 512))]
        for t in range(4)
    ]

    def chunk(half, i):
        return pl.ds(half * 512 + i * PART, PART)

    class RingSum:
        def __init__(self, at, landing, to, i):
            self.rows = [chunk(half, i) for half in range(2)]
            self.x, self.y, self.z = [], [], []
            for half in range(2):
                r = self.rows[half]
                ahead, back = (UP, DOWN) if half == 0 else (DOWN, UP)
                d = 1 - 2 * half
                self.x.append(copy(at(FAR, r), landing.at[0, r], to(d)))
                self.z.append(copy(at(ahead, r), landing.at[1, r], to(d)))
                self.y.append(copy(at(back, r), landing.at[2, r], to(-d)))

    PAIRS = 2
    places = [(pb + d) % 4 for d in offsets]
    rs1 = [RingSum(lambda t, r: cent.at[t, r], recv1, on_a, i) for i in range(PAIRS)]
    direct = [
        [
            copy(part1.at[places[t], chunk(half, i)], recv2.at[t, chunk(half, i)], on_b(offsets[t]))
            for t in (FAR, UP, DOWN)
            for half in range(2)
        ]
        for i in range(PAIRS)
    ]

    def start_both(copies):
        for c in copies:
            c.start()

    def make_half(t):
        for i in range(2):
            partial_sum(4 + t, pb + offsets[t], 1 - core, i)
            halves[t][i].start()
        for i in range(2):
            partial_sum(t, pa + offsets[t], core, i)

    def merge(t, half):
        halves[t][half].wait_recv()

        @pl.loop(2 * half, 2 * half + 2)
        def _(i):
            came = land[pl.ds(pl.multiple_of(t * COLS + i * 256, 256), 256), pl.ds(0, HALF)]
            cent[t, quarter(i), :] = add(cent[t, quarter(i), :], came).astype(BF16)

    ones = jnp.ones((8, ROWS), BF16)
    count[0] = dot(ones, assign_t[...], 1, 1)
    count_s = copy(count.at[0], count.at[1], sibling)
    count_a = [copy(count.at[2], count.at[3 + i], on_a(d)) for i, d in enumerate((1, -1, 2))]
    count_b = [copy(count.at[6], count.at[7 + i], on_b(d)) for i, d in enumerate((1, -1, 2))]

    pl.semaphore_wait(free_sem, 1)
    make_half(FAR)
    for half in range(2):
        merge(FAR, half)
        rs1[0].x[half].start()
        rs1[1].x[half].start()
    count_s.start()
    make_half(UP)
    make_half(DOWN)
    for t in (UP, DOWN):
        for half in range(2):
            merge(t, half)
    start_both(rs1[0].y)

    def turn1(i):
        for half, t in ((0, UP), (1, DOWN)):
            r = rs1[i].rows[half]
            rs1[i].x[half].wait_recv()
            cent[t, r, :] = add(cent[t, r, :], recv1[0, r, :]).astype(BF16)
            rs1[i].z[half].start()

    def end1(i):
        for half in range(2):
            r = rs1[i].rows[half]
            rs1[i].y[half].wait_recv()
            rs1[i].z[half].wait_recv()
            total = add(cent[OWN, r, :], recv1[1, r, :], recv1[2, r, :]).astype(BF16)
            for b in range(4):
                part1[b, r, :] = total[:, b * 128 : (b + 1) * 128]
        start_both(direct[i])

    send_out = [
        [copy(out_v.at[:, chunk(half, i)], out_hbm.at[:, chunk(half, i)], swap, is_away) for half in range(2)]
        for i in range(PAIRS)
    ]
    store_out = [
        [pltpu.make_async_copy(out_v.at[:, chunk(half, i)], out_hbm.at[:, chunk(half, i)], local_sem.at[16 + 2 * i + half])
         for half in range(2)]
        for i in range(PAIRS)
    ]

    def end2(i):
        for c in direct[i]:
            c.wait_recv()
        for half in range(2):
            r = chunk(half, i)
            sums = add(part1[pb, r, :], recv2[0, r, :], recv2[1, r, :], recv2[2, r, :])
            counts = count[6, 0:1, r] + count[7, 0:1, r] + count[8, 0:1, r] + count[9, 0:1, r]
            out_v[:, r] = sums.T / jnp.maximum(counts, 1.0)
            when(is_home, store_out[i][half].start)
            when(is_away, send_out[i][half].start)

    turn1(0)
    start_both(rs1[1].y)
    count_s.wait_recv()
    count[2] = count[0] + count[1]
    start_both(count_a)
    make_half(OWN)
    turn1(1)

    @pl.when(is_away)
    def _():
        swap_desc[0].wait_send()
        swap_desc[1].wait_send()

    @pl.loop(0, 6)
    def _(i):
        s = pl.ds(pl.multiple_of(i * 128, 128), 128)
        desc[0, s, :] = assign_t[:, s].T

    store_assign = pltpu.make_async_copy(desc.at[0], assign_hbm, local_sem.at[14])
    send_assign = copy(desc.at[0], assign_hbm, swap, is_away)
    when(is_home, store_assign.start)
    when(is_away, send_assign.start)
    for c in count_a:
        c.wait_recv()
    count[6] = count[2] + count[3] + count[4] + count[5]
    start_both(count_b)
    merge(OWN, 0)
    merge(OWN, 1)
    end1(0)
    for c in count_b:
        c.wait_recv()
    end1(1)
    end2(0)
    end2(1)

    for c, cond in started:
        if any(c is d for d in swap_desc):
            continue
        if cond is None:
            c.wait_send()
        else:
            when(cond, lambda c=c: c.wait_send())

    @pl.when(is_home)
    def _():
        store_assign.wait()
        for pair in store_out:
            for c in pair:
                c.wait()

    @pl.when(is_away)
    def _():
        send_assign.wait_recv()
        for pair in send_out:
            for c in pair:
                c.wait_recv()


def per_device(descriptors, landmarks, whitening, centroids):
    vmem = pltpu.VMEM
    hbm = pl.BlockSpec(memory_space=pl.ANY)
    flops = 2 * ROWS * LAND * DEPTH * 4
    return pl.pallas_call(
        body,
        out_shape=(
            jax.ShapeDtypeStruct((ROWS, COLS), BF16),
            jax.ShapeDtypeStruct((BLOCK, COLS), F32),
        ),
        in_specs=[hbm] * 4,
        out_specs=(hbm, hbm),
        scratch_shapes=[
            vmem((2, ROWS, DEPTH), BF16),
            vmem((BLOCK, DEPTH), BF16),
            vmem((CHUNKS, BLOCK, PIECE), BF16),
            vmem((LAND, DEPTH), BF16),
            vmem((WCHUNKS, LAND, PIECE), BF16),
            vmem((ROWS, LAND), BF16),
            vmem((16, ROWS, PIECE), BF16),
            vmem((8, COLS, HALF), BF16),
            vmem((COLS, ROWS), F32),
            vmem((COLS, ROWS), BF16),
            vmem((3, COLS, HALF), BF16),
            vmem((4, COLS, 128), BF16),
            vmem((3, COLS, 128), BF16),
            vmem((4, 8, ROWS), F32),
            vmem((10, 8, COLS), F32),
            vmem((BLOCK, COLS), F32),
            pltpu.SemaphoreType.DMA((NSEM,)),
            pltpu.SemaphoreType.DMA((NSEM,)),
            pltpu.SemaphoreType.DMA((20,)),
            pltpu.SemaphoreType.REGULAR,
        ],
        compiler_params=pltpu.CompilerParams(
            collective_id=0, has_side_effects=True, vmem_limit_bytes=62 << 20
        ),
        cost_estimate=pl.CostEstimate(flops=flops, bytes_accessed=16 << 20, transcendentals=0),
        name="kmeans_step",
    )(descriptors, landmarks, whitening, centroids)


def solution(mesh):
    in_specs = (P("blk", None), P("blk", None), P("blk", "cent"), P("cent", None))
    out_specs = (P("blk", "cent"), P("blk", "cent"))
    return jax.shard_map(
        per_device, mesh=mesh, in_specs=in_specs, out_specs=out_specs, check_vma=False
    )
```

time: 177 us -> 147 us (0.83); the launches traced: 175 us -> 147 us
  Pallas kernels: 171 us -> 142 us
    pallas_call x1, Pallas kernels: 171 us -> 142 us  [per_device(): pl.pallas_call(body, out_shape=(jax.ShapeDtypeStruct((ROWS, COLS), BF16),...]
where the time goes in v2:
time: 147 us
  Pallas kernels  142 us (97%)
  local copies, waits for them, and re-layouts  3.52 us (2%)
    pallas_call x1, Pallas kernels, per_device(): pl.pallas_call(body, out_shape=(jax.ShapeDtypeStruct((ROWS, COLS), BF16),...  142 us
    unnamed x4, local copies, waits for them, and re-layouts  3.52 us

profile of v2, /device:TPU:1, one launch (start us, length us, event | category | flops | bytes accessed | tf_op | source)
XLA Modules:
  0.0 146.6 jit_solution(15290588427955597736)
XLA Ops:
  0.6 142.4 %kmeans_step.1 = (bf16[768,1024]{1,0:T(8,128)(2,1)}, f32[128,1024]{1,0:T(8,128)}) custom-call(bf16[768,1024]{1,0:T(8,128)(2,1)} %desc_hbm.1, bf16[128,1024]{1,0:T(8,128)(2,1)} %land_hbm.1, bf16[128,1024]{1,0:T(8,128)(2,1)} %white_hbm.1, bf16[1024,4096]{1,0:T(8,128)(2,1)} %cent_hbm.1), custom_call_target="tpu_custom_call" | custom-call | flops 25769803776 | bytes 16777216 | tf_op jit(solution)/shard_map/kmeans_step/pallas_call | solution.py:653
  143.1 0.0 copy-start
  143.1 2.7 %copy.8 = bf16[768,1024]{1,0:T(8,128)(2,1)} copy(bf16[768,1024]{1,0:T(8,128)(2,1)} %get-tuple-element.4) | data formatting | bytes 3145728
  145.8 0.0 copy-done
  145.8 0.8 copy.9
Async XLA Ops:
  143.1 2.7 %copy-start = (f32[128,1024]{1,0:T(8,128)S(1)}, f32[128,1024]{1,0:T(8,128)}, u32[]{:S(2)}) copy-start(f32[128,1024]{1,0:T(8,128)} %get-tuple-element.5) | copy-start | bytes 1572868

commit v3 on v2

--- a/solution.py
+++ b/solution.py
@@ -24,7 +24,8 @@
 WCHUNKS = 8
 PART = 256
 COLS = 1024
-NSEM = 224
+NSEND = 64
+NRECV = 116
 
 
 def dot(a, b, ca, cb):
@@ -70,28 +71,62 @@
     y_far, y_far_sib = device(x, y + 2, z, core), device(x, y + 2, z, core + 1)
     y_pair, other_same = device(x, swap_y, z, core), device(x, 7 - y, z, core)
 
-    started = []
+    free_sends = list(range(NSEND))[::-1]
     counter = [0]
-
-    def wait_send(c):
-        for i, (other_copy, cond) in enumerate(started):
-            if other_copy is c:
-                del started[i]
-                if cond is None:
-                    c.wait_send()
-                else:
-                    pl.when(cond)(c.wait_send)
-                return
-
-    def copy(src, dst, target, cond=None):
-        k = counter[0]
+    live = []
+
+    def new_recv():
         counter[0] += 1
-        c = pltpu.make_async_remote_copy(
-            src_ref=src, dst_ref=dst, send_sem=send_sem.at[k], recv_sem=recv_sem.at[k],
+        return counter[0] - 1
+
+    def describe(src, dst, send, recv, target):
+        return pltpu.make_async_remote_copy(
+            src_ref=src, dst_ref=dst, send_sem=send_sem.at[send], recv_sem=recv_sem.at[recv],
             device_id=target, device_id_type=MESH,
         )
-        started.append((c, cond))
-        return c
+
+    class Copy:
+        def __init__(self, src, dst, target, cond=None, recv=None):
+            self.parts = src, dst
+            self.target, self.cond = target, cond
+            self.recv = new_recv() if recv is None else recv
+
+        def start(self):
+            self.send = free_sends.pop()
+            live.append(self)
+            describe(*self.parts, self.send, self.recv, self.target).start()
+
+        def wait_recv(self):
+            describe(*self.parts, 0, self.recv, self.target).wait_recv()
+
+        def wait_send(self):
+            wait = describe(*self.parts, self.send, self.recv, self.target).wait_send
+            if self.cond is None:
+                wait()
+            else:
+                pl.when(self.cond)(wait)
+            live.remove(self)
+            free_sends.append(self.send)
+
+    class Group(Copy):
+        def __init__(self, members, whole, target, cond=None):
+            super().__init__(*whole, target, cond)
+            self.members = members
+            self.left = len(members)
+
+        def start(self, i=None):
+            if self.left == len(self.members):
+                self.send = free_sends.pop()
+                live.append(self)
+            for src, dst, target in self.members if i is None else [self.members[i]]:
+                self.left -= 1
+                describe(src, dst, self.send, self.recv, target).start()
+
+    copy = Copy
+
+    def retire(copies):
+        for c in copies:
+            c.wait_send()
 
     def when(cond, f):
         pl.when(cond)(f)
@@ -129,9 +164,12 @@
 
     swap_land = copy(seed.at[mine], land.at[pl.ds(HALF_B, SUB)], y_pair)
 
+    widths = (CHUNKS, WCHUNKS - CHUNKS)
+
     def white_seed(quarter, part, rows, target, cond):
         return copy(
-            wseed.at[:, rows], white.at[pl.ds(quarter * CHUNKS, CHUNKS), pl.ds(part * HALF_B, SUB)], target, cond
+            wseed.at[pl.ds(0, widths[quarter]), rows],
+            white.at[pl.ds(quarter * CHUNKS, widths[quarter]), pl.ds(part * HALF_B, SUB)], target, cond,
         )
 
     seed_own = pltpu.make_async_copy(
@@ -145,25 +183,28 @@
     seed_other = white_seed(1, 1, theirs, other, is_away)
     seed_other_same = white_seed(1, 1, mine, other_same, is_away)
     CUT = 256
-    share_cent = [
-        copy(cent_hbm.at[:, pl.ds(p * HALF, HALF)], cent.at[p], sibling, is_home) for p in range(8)
-    ]
+    share_cent = Group(
+        [(cent_hbm.at[:, pl.ds(p * HALF, HALF)], cent.at[p], sibling) for p in range(8)],
+        (cent, cent), sibling, is_home,
+    )
     swap_desc = [
         copy(desc.at[0, pl.ds(0, CUT)], desc.at[1, pl.ds(0, CUT)], swap, is_away),
         copy(desc.at[0, pl.ds(CUT, ROWS - CUT)], desc.at[1, pl.ds(CUT, ROWS - CUT)], other, is_away),
     ]
 
     class Ring:
-        def __init__(self, at, size, to):
-            def go(src, dst, rows, half, d):
-                lo = half * (rows // 2)
-                n = rows if half == 0 and dst != 2 else rows // 2
-                return copy(at(src, lo, n), at(dst, lo, n), to(d))
-
-            self.up = go(0, 3, size, 0, 1)
-            self.down = go(0, 1, size, 0, -1)
-            self.fwd_up = go(3, 2, size, 0, 1)
-            self.fwd_down = go(1, 2, size, 1, -1)
+        def __init__(self, at, size, to, direct=False):
+            half = size // 2
+            self.up = copy(at(0, 0, size), at(3, 0, size), to(1))
+            self.down = copy(at(0, 0, size), at(1, 0, size), to(-1))
+            if direct:
+                self.far = copy(at(0, 0, size), at(2, 0, size), to(2))
+                self.copies = [self.up, self.down, self.far]
+                return
+            self.fwd_up = copy(at(3, 0, half), at(2, 0, half), to(1))
+            self.fwd_down = copy(at(1, half, half), at(2, half, half), to(-1), recv=self.fwd_up.recv)
+            self.both = copy(at(0, 0, size), at(2, 0, size), to(1), recv=self.fwd_up.recv)
+            self.copies = [self.up, self.down, self.fwd_up, self.fwd_down]
 
         def start(self):
             self.up.start()
@@ -176,8 +217,7 @@
             self.fwd_down.start()
 
         def finish(self):
-            self.fwd_up.wait_recv()
-            self.fwd_down.wait_recv()
+            self.both.wait_recv()
 
     def land_a(part):
         return lambda slot, lo, n: land.at[pl.ds(part * HALF_B + slot * SUB + lo, n)]
@@ -187,25 +227,29 @@
 
     def white_a(quarter, part):
         return lambda slot, lo, n: white.at[
-            pl.ds(quarter * CHUNKS, CHUNKS), pl.ds(part * HALF_B + slot * SUB + lo, n)
+            pl.ds(quarter * CHUNKS, widths[quarter]), pl.ds(part * HALF_B + slot * SUB + lo, n)
         ]
 
     def white_b(k):
         return lambda slot, lo, n: white.at[k, pl.ds(slot * GROUP + lo, n)]
 
-    def to_sibling(at, slot):
-        return copy(at(slot, 0, GROUP), at(4 + slot, 0, GROUP), sibling)
-
-    la = [Ring(land_a(part), SUB, on_a) for part in range(2)]
+    la = [Ring(land_a(part), SUB, on_a, True) for part in range(2)]
     lb = [Ring(land_b(s * SUB), SUB, on_b) for s in range(4)]
     lb_rest = Ring(land_b(HALF_B), HALF_B, on_b)
     wa = [[Ring(white_a(q, part), SUB, on_a) for part in range(2)] for q in range(2)]
     wb = [Ring(white_b(k), GROUP, on_b) for k in range(WCHUNKS)]
-    ls = [to_sibling(land_b(0), s) for s in range(4)]
-    ws = [[to_sibling(white_b(k), s) for s in range(4)] for k in range(WCHUNKS)]
+    ls = [copy(land_b(0)(s, 0, GROUP), land_b(0)(4 + s, 0, GROUP), sibling) for s in range(4)]
+    ws = [
+        Group(
+            [(white_b(k)(s, 0, GROUP), white_b(k)(4 + s, 0, GROUP), sibling) for s in range(4)],
+            (white_b(k)(0, 0, 4 * GROUP), white_b(k)(4, 0, 4 * GROUP)), sibling,
+        )
+        for k in range(WCHUNKS)
+    ]
 
     swap_land.start()
     la[0].start()
+    la[0].far.start()
     lb[0].start()
     for c in load_white:
         c.wait()
@@ -238,8 +282,9 @@
     def _():
         seed_far.start()
         seed_far_sib.start()
-        for c in load_cent + share_cent:
+        for c in load_cent:
             c.start()
+        share_cent.start()
 
     sharpness = math.sqrt(DEPTH)
 
@@ -249,36 +294,37 @@
         kern[:, cols] = jnp.exp(sharpness * cosine).astype(BF16)
 
     la[0].up.wait_recv()
-    la[0].fwd_up.start()
     lb[3].start()
     la[0].down.wait_recv()
-    la[0].fwd_down.start()
     lb[1].start()
+    la[0].far.wait_recv()
+    lb[2].start()
     swap_land.wait_recv()
     la[1].start()
+    la[1].far.start()
     lb[0].forward()
-    la[0].finish()
-    lb[2].start()
+
+    @pl.when(is_home)
+    def _():
+        seed_own.wait()
+        seed_pair.wait_recv()
+
+    @pl.when(is_away)
+    def _():
+        seed_sib.wait_recv()
+        seed_swap.wait_recv()
+
+    for ring in wa[0]:
+        ring.start()
+    for c in la[1].copies:
+        c.wait_recv()
+    lb_rest.start()
+    ls[0].start()
     lb[3].forward()
     lb[1].forward()
-    la[1].forward()
-
-    @pl.when(is_home)
-    def _():
-        seed_own.wait()
-        seed_pair.wait_recv()
-
-    @pl.when(is_away)
-    def _():
-        seed_sib.wait_recv()
-        seed_swap.wait_recv()
-
+    lb[2].forward()
     for ring in wa[0]:
-        ring.start()
-    lb[2].forward()
-    la[1].finish()
-    lb_rest.start()
-    ls[0].start()
+        ring.forward()
 
     @pl.when(is_away)
     def _():
@@ -286,8 +332,6 @@
         swap_desc[1].wait_recv()
 
     kernel_group(0)
-    for ring in wa[0]:
-        ring.forward()
     for ring in lb:
         ring.finish()
     lb_rest.forward()
@@ -298,20 +342,20 @@
 
     def start_white(k):
         wb[k].start()
-        ws[k][0].start()
+        ws[k].start(0)
 
     def forward_white(k):
         wb[k].forward()
-        ws[k][3].start()
-        ws[k][1].start()
+        ws[k].start(3)
+        ws[k].start(1)
 
     def finish_white(k):
         wb[k].finish()
-        ws[k][2].start()
+        ws[k].start(2)
 
     start_white(0)
+    kernel_group(3)
     start_white(1)
-    kernel_group(3)
     kernel_group(1)
     lb_rest.finish()
     ls[2].start()
@@ -338,6 +382,8 @@
     kernel_group(5)
     kernel_group(2)
     finish_white(0)
+    retire([swap_land, seed_sib, seed_pair, seed_swap, seed_far, seed_far_sib, seed_other, seed_other_same])
+    retire([c for ring in la + lb + [lb_rest] + wa[0] for c in ring.copies])
     for ring in wa[1]:
         ring.forward()
     forward_white(1)
@@ -349,8 +395,7 @@
         return ((y + r) % 4) * CHUNKS + k
 
     def features(k):
-        for s in range(4):
-            ws[k][s].wait_recv()
+        ws[k].wait_recv()
         slot = slot_of(0, k) if k < CHUNKS else slot_of(2, k - CHUNKS)
 
         @pl.loop(0, 3)
@@ -358,23 +403,32 @@
             s = pl.ds(pl.multiple_of(i * 256, 256), 256)
             feat[slot, s, :] = dot(kern[s, :], white[k], 1, 0).astype(BF16)
 
+        if k > 0:
+            retire(wb[k - 1].copies + [ws[k - 1]])
+
     own = [feat.at[slot_of(0, k)] for k in range(CHUNKS)]
     f_up = [copy(own[k], own[k], y_up) for k in range(CHUNKS)]
     f_down = [copy(own[k], own[k], y_down) for k in range(CHUNKS)]
 
-    def logits(r, k):
-        if r == 1:
-            f_down[k].wait_recv()
-        if r == 3:
-            f_up[k].wait_recv()
-        lanes = pl.ds((k % 2) * PIECE, PIECE)
-        slot, piece = ((y + r) % 4) * 2 + k // 2, slot_of(r, k)
+    begun = []
+
+    def logits(pieces):
+        terms = []
+        for r, k in pieces:
+            if r == 1:
+                f_down[k].wait_recv()
+            if r == 3:
+                f_up[k].wait_recv()
+            lanes = pl.ds((k % 2) * PIECE, PIECE)
+            terms.append((((y + r) % 4) * 2 + k // 2, lanes, slot_of(r, k)))
+        fresh = not begun
+        begun.append(True)
 
         @pl.loop(0, 2)
         def _(i):
             s = pl.ds(pl.multiple_of(i * 512, 512), 512)
-            update = dot(cent[slot, s, lanes], feat[piece], 1, 1)
-            if k == 0 and r == 0:
+            update = sum(dot(cent[slot, s, lanes], feat[piece], 1, 1) for slot, lanes, piece in terms)
+            if fresh:
                 logit[s, :] = update
             else:
                 logit[s, :] += update
@@ -388,7 +442,8 @@
             for ring in wa[1]:
                 ring.finish()
         forward_white(k + 1)
-        start_white(k + 3)
+        if k + 3 < WCHUNKS:
+            start_white(k + 3)
         features(k)
         f_up[k].start()
         f_down[k].start()
@@ -400,30 +455,28 @@
 
     @pl.when(is_away)
     def _():
-        for c in share_cent:
-            c.wait_recv()
-
-    todo = [
-        [(0, 0), (0, 1)],
-        [(0, 2), (0, 3), (2, 0)],
-        [(1, 0), (3, 0), (2, 1)],
-        [(1, 1), (3, 1), (2, 2), (1, 2), (3, 2), (2, 3), (1, 3), (3, 3)],
-    ]
+        share_cent.wait_recv()
+
+    early = {7: [[(2, 1), (2, 2)]]}
+    late = {
+        4: [[(0, 0), (0, 1)], [(0, 2), (0, 3)]],
+        5: [[(1, 0), (3, 0), (2, 0)]],
+        6: [[(1, 1), (3, 1)]],
+        7: [[(1, 2), (3, 2)], [(1, 3), (3, 3), (2, 3)]],
+    }
     for k in range(CHUNKS, WCHUNKS):
         finish_white(k)
         if k + 1 < WCHUNKS:
             forward_white(k + 1)
         if k + 3 < WCHUNKS:
             start_white(k + 3)
+        for pieces in early.get(k, ()):
+            logits(pieces)
         features(k)
-        for r, piece in todo[k - CHUNKS]:
-            logits(r, piece)
-
-    for ring in la + lb + [lb_rest]:
-        for c in (ring.up, ring.down, ring.fwd_up, ring.fwd_down):
-            wait_send(c)
-    for c in ls:
-        wait_send(c)
+        for pieces in late.get(k, ()):
+            logits(pieces)
+
+    retire(ls)
     pl.semaphore_signal(free_sem, inc=1, device_id=sibling, device_id_type=MESH)
 
     def quarter(i):
@@ -442,14 +495,12 @@
     total = lax.fori_loop(0, 4, exponentials, jnp.zeros((1, ROWS), F32))
     stat[0, 0:1, :] = top
     stat[0, 1:2, :] = total
-    stat_copies = [
-        copy(stat.at[0], stat.at[i + 1], target)
-        for i, target in enumerate((y_up, y_down, y_far))
-    ]
-    for c in stat_copies:
-        c.start()
-    for c in stat_copies:
-        c.wait_recv()
+    share_stat = Group(
+        [(stat.at[0], stat.at[i + 1], target) for i, target in enumerate((y_up, y_down, y_far))],
+        (stat.at[pl.ds(1, 3)], stat.at[pl.ds(1, 3)]), y_up,
+    )
+    share_stat.start()
+    share_stat.wait_recv()
     tops = [stat[i, 0:1, :] for i in range(4)]
     all_top = jnp.maximum(jnp.maximum(tops[0], tops[1]), jnp.maximum(tops[2], tops[3]))
     all_total = sum(stat[i, 1:2, :] * jnp.exp(tops[i] - all_top) for i in range(4))
@@ -502,12 +553,16 @@
     PAIRS = 2
     places = [(pb + d) % 4 for d in offsets]
     rs1 = [RingSum(lambda t, r: cent.at[t, r], recv1, on_a, i) for i in range(PAIRS)]
+    same_size = recv2.at[:, pl.ds(0, 2 * PART)]
     direct = [
-        [
-            copy(part1.at[places[t], chunk(half, i)], recv2.at[t, chunk(half, i)], on_b(offsets[t]))
-            for t in (FAR, UP, DOWN)
-            for half in range(2)
-        ]
+        Group(
+            [
+                (part1.at[places[t], chunk(half, i)], recv2.at[t, chunk(half, i)], on_b(offsets[t]))
+                for t in (FAR, UP, DOWN)
+                for half in range(2)
+            ],
+            (same_size, same_size), on_b(1),
+        )
         for i in range(PAIRS)
     ]
 
@@ -533,8 +588,9 @@
     ones = jnp.ones((8, ROWS), BF16)
     count[0] = dot(ones, assign_t[...], 1, 1)
     count_s = copy(count.at[0], count.at[1], sibling)
-    count_a = [copy(count.at[2], count.at[3 + i], on_a(d)) for i, d in enumerate((1, -1, 2))]
-    count_b = [copy(count.at[6], count.at[7 + i], on_b(d)) for i, d in enumerate((1, -1, 2))]
+    three = count.at[pl.ds(3, 3)], count.at[pl.ds(3, 3)]
+    count_a = Group([(count.at[2], count.at[3 + i], on_a(d)) for i, d in enumerate((1, -1, 2))], three, on_a(1))
+    count_b = Group([(count.at[6], count.at[7 + i], on_b(d)) for i, d in enumerate((1, -1, 2))], three, on_b(1))
 
     pl.semaphore_wait(free_sem, 1)
     make_half(FAR)
@@ -565,12 +621,16 @@
             total = add(cent[OWN, r, :], recv1[1, r, :], recv1[2, r, :]).astype(BF16)
             for b in range(4):
                 part1[b, r, :] = total[:, b * 128 : (b + 1) * 128]
-        start_both(direct[i])
-
-    send_out = [
-        [copy(out_v.at[:, chunk(half, i)], out_hbm.at[:, chunk(half, i)], swap, is_away) for half in range(2)]
-        for i in range(PAIRS)
-    ]
+        direct[i].start()
+
+    send_out = Group(
+        [
+            (out_v.at[:, chunk(half, i)], out_hbm.at[:, chunk(half, i)], swap)
+            for i in range(PAIRS)
+            for half in range(2)
+        ],
+        (out_v, out_hbm), swap, is_away,
+    )
     store_out = [
         [pltpu.make_async_copy(out_v.at[:, chunk(half, i)], out_hbm.at[:, chunk(half, i)], local_sem.at[16 + 2 * i + half])
          for half in range(2)]
@@ -578,28 +638,24 @@
     ]
 
     def end2(i):
-        for c in direct[i]:
-            c.wait_recv()
+        direct[i].wait_recv()
         for half in range(2):
             r = chunk(half, i)
             sums = add(part1[pb, r, :], recv2[0, r, :], recv2[1, r, :], recv2[2, r, :])
             counts = count[6, 0:1, r] + count[7, 0:1, r] + count[8, 0:1, r] + count[9, 0:1, r]
             out_v[:, r] = sums.T / jnp.maximum(counts, 1.0)
             when(is_home, store_out[i][half].start)
-            when(is_away, send_out[i][half].start)
+            when(is_away, lambda: send_out.start(2 * i + half))
 
     turn1(0)
     start_both(rs1[1].y)
     count_s.wait_recv()
     count[2] = count[0] + count[1]
-    start_both(count_a)
+    count_a.start()
     make_half(OWN)
     turn1(1)
 
-    @pl.when(is_away)
-    def _():
-        swap_desc[0].wait_send()
-        swap_desc[1].wait_send()
+    retire(swap_desc)
 
     @pl.loop(0, 6)
     def _(i):
@@ -610,26 +666,18 @@
     send_assign = copy(desc.at[0], assign_hbm, swap, is_away)
     when(is_home, store_assign.start)
     when(is_away, send_assign.start)
-    for c in count_a:
-        c.wait_recv()
+    count_a.wait_recv()
     count[6] = count[2] + count[3] + count[4] + count[5]
-    start_both(count_b)
+    count_b.start()
     merge(OWN, 0)
     merge(OWN, 1)
     end1(0)
-    for c in count_b:
-        c.wait_recv()
+    count_b.wait_recv()
     end1(1)
     end2(0)
     end2(1)
 
-    for c, cond in started:
-        if any(c is d for d in swap_desc):
-            continue
-        if cond is None:
-            c.wait_send()
-        else:
-            when(cond, lambda c=c: c.wait_send())
+    retire(list(live))
 
     @pl.when(is_home)
     def _():
@@ -641,21 +689,20 @@
     @pl.when(is_away)
     def _():
         send_assign.wait_recv()
-        for pair in send_out:
-            for c in pair:
-                c.wait_recv()
+        send_out.wait_recv()
 
 
 def per_device(descriptors, landmarks, whitening, centroids):
     vmem = pltpu.VMEM
     hbm = pl.BlockSpec(memory_space=pl.ANY)
     flops = 2 * ROWS * LAND * DEPTH * 4
+    shapes = (
+        jax.ShapeDtypeStruct((ROWS, COLS), BF16),
+        jax.ShapeDtypeStruct((BLOCK, COLS), F32),
+    )
     return pl.pallas_call(
         body,
-        out_shape=(
-            jax.ShapeDtypeStruct((ROWS, COLS), BF16),
-            jax.ShapeDtypeStruct((BLOCK, COLS), F32),
-        ),
+        out_shape=shapes,
         in_specs=[hbm] * 4,
         out_specs=(hbm, hbm),
         scratch_shapes=[
@@ -675,8 +722,8 @@
             vmem((4, 8, ROWS), F32),
             vmem((10, 8, COLS), F32),
             vmem((BLOCK, COLS), F32),
-            pltpu.SemaphoreType.DMA((NSEM,)),
-            pltpu.SemaphoreType.DMA((NSEM,)),
+            pltpu.SemaphoreType.DMA((NSEND,)),
+            pltpu.SemaphoreType.DMA((NRECV,)),
             pltpu.SemaphoreType.DMA((20,)),
             pltpu.SemaphoreType.REGULAR,
         ],

time: 147 us -> 141 us (0.959)
  Pallas kernels: 142 us -> 137 us
    pallas_call x1, Pallas kernels: 142 us -> 137 us  [per_device(): pl.pallas_call(body, out_shape=shapes, in_specs=[hbm] * 4, out_specs=(hbm...]
where the time goes in v3:
time: 141 us
  Pallas kernels  137 us (97%)
  local copies, waits for them, and re-layouts  3.52 us (2%)
    pallas_call x1, Pallas kernels, per_device(): pl.pallas_call(body, out_shape=shapes, in_specs=[hbm] * 4, out_specs=(hbm...  137 us
    unnamed x4, local copies, waits for them, and re-layouts  3.52 us

profile of v3, /device:TPU:1, one launch (start us, length us, event | category | flops | bytes accessed | tf_op | source)
XLA Modules:
  0.0 140.9 jit_solution(9268821221733181155)
XLA Ops:
  0.6 136.7 %kmeans_step.1 = (bf16[768,1024]{1,0:T(8,128)(2,1)}, f32[128,1024]{1,0:T(8,128)}) custom-call(bf16[768,1024]{1,0:T(8,128)(2,1)} %desc_hbm.1, bf16[128,1024]{1,0:T(8,128)(2,1)} %land_hbm.1, bf16[128,1024]{1,0:T(8,128)(2,1)} %white_hbm.1, bf16[1024,4096]{1,0:T(8,128)(2,1)} %cent_hbm.1), custom_call_target="tpu_custom_call" | custom-call | flops 25769803776 | bytes 16777216 | tf_op jit(solution)/shard_map/kmeans_step/pallas_call | solution.py:703
  137.4 0.0 copy-start
  137.4 2.7 %copy.8 = bf16[768,1024]{1,0:T(8,128)(2,1)} copy(bf16[768,1024]{1,0:T(8,128)(2,1)} %get-tuple-element.4) | data formatting | bytes 3145728
  140.1 0.0 copy-done
  140.1 0.8 copy.9
Async XLA Ops:
  137.4 2.7 %copy-start = (f32[128,1024]{1,0:T(8,128)S(1)}, f32[128,1024]{1,0:T(8,128)}, u32[]{:S(2)}) copy-start(f32[128,1024]{1,0:T(8,128)} %get-tuple-element.5) | copy-start | bytes 1572868
